TPU v7x, 32 devices: a whole 2x2x4 slice. The times are simulated.
32 devices in a mesh: seq: 16 (over z, y, x), kmer: 2 (over core).
Axes of the slice: x: 2, y: 2, z: 4, core: 2. Of those that a mesh axis runs over, the one named last changes fastest.
Arguments:
- profiles: bfloat16 [2048, 16384], P(('seq', 'kmer')), may hold values from -6 to 6
- lengths: int32 [16384], P('seq'), may hold values from 64 to 1024
- owners: int32 [2], replicated, may hold values from 0 to 15
- block_mask: int32 [2, 128, 8], P(None, 'seq'), may hold values 0 or 1
Outputs:
- scores: bfloat16 [16384, 2, 1024], P('seq', None, 'kmer')
All inputs are finite; a program needn't handle non-finite values. No bound on the sum of `block_mask` on one device may be relied on, other than what follows from the above.
Results may differ from a plain program's by a relative error of at most 0.001.
Values may be sent and summed in bfloat16 or wider, within the bound.
A program may use at most 64 MiB of HBM per device.

v0:
```python
import jax
import jax.numpy as jnp
from jax import lax
from jax.sharding import PartitionSpec as P

KM = 2048
BLK = 128
SECTIONS = 2


def broadcast(block, axis, source):
    block = jnp.where(lax.axis_index(axis) == source, block, jnp.zeros_like(block))
    return lax.psum(block, axis)


def shards(profiles, lengths, owners, block_mask):
    local = lax.all_to_all(profiles, "seq", split_axis=1, concat_axis=0, tiled=True)
    panel_rows = local.shape[1]
    half = panel_rows // 2
    part = lax.axis_index("kmer")
    row_len = lengths.astype(jnp.float32)
    scale = 256.0 / jnp.sqrt(jnp.float32(KM))
    contract = (((0,), (0,)), ((), ()))
    outs = []
    for section in range(SECTIONS):
        panel, panel_len = (
            broadcast(local, "seq", owners[section]),
            broadcast(lengths, "seq", owners[section]),
        )
        partial_value = lax.dot_general(local, panel, contract, preferred_element_type=jnp.float32)
        raw = lax.psum_scatter(partial_value, "kmer", scatter_dimension=1, tiled=True)
        col_len = lax.dynamic_slice_in_dim(panel_len.astype(jnp.float32), part * half, half, 0)
        mask_full = jnp.repeat(jnp.repeat(block_mask[section], BLK, axis=0), BLK, axis=1).astype(
            jnp.float32
        )
        mask = lax.dynamic_slice_in_dim(mask_full, part * half, half, 1)
        norm = scale * lax.rsqrt(row_len[:, None] * col_len[None, :])
        outs.append((raw * norm * mask).astype(jnp.bfloat16))
    return jnp.stack(outs, axis=1)


def solution(mesh):
    placed = (P(("seq", "kmer"), None), P("seq"), P(), P(None, "seq", None))
    return jax.shard_map(
        shards, mesh=mesh, in_specs=placed, out_specs=P("seq", None, "kmer"), check_vma=False
    )
```

profile of v0, /device:TPU:0, one launch (start us, length us, event | category | flops | bytes accessed | tf_op | source)
XLA Modules:
  0.0 284.3 jit_solution(8269700664513439694)
XLA Ops:
  6.5 3.1 %copy.13 = bf16[8,16,8,1024]{3,2,0,1:T(8,128)(2,1)} copy(bf16[8,16,8,1024]{3,2,1,0:T(8,128)(2,1)} %bitcast.38) | data formatting | bytes 4194304 | tf_op jit(solution)/shard_map/all_to_all | solution.py:17
  9.7 0.0 copy-start.4
  9.7 8.4 %all-to-all-start = ((bf16[64,16,1024]{2,0,1:T(8,128)(2,1)}), bf16[64,16,1024]{2,0,1:T(8,128)(2,1)S(1)}, u32[]{:S(2)}, u32[]{:S(2)}) async-start(bf16[64,16,1024]{2,0,1:T(8,128)(2,1)} %bitcast.37), calls=%async_computation | async-start | bytes 4194304 | tf_op jit(solution)/shard_map/all_to_all | solution.py:17
  18.1 0.0 all-reduce.4.cloned.1.call-start
  18.2 0.0 copy-done.4
  18.2 0.6 fusion.3
  20.0 41.2 %all-to-all-done = bf16[64,16,1024]{2,0,1:T(8,128)(2,1)S(1)} async-done(((bf16[64,16,1024]{2,0,1:T(8,128)(2,1)}), bf16[64,16,1024]{2,0,1:T(8,128)(2,1)S(1)}, u32[]{:S(2)}, u32[]{:S(2)}) %all-to-all-start) | async-done | bytes 2097184 | tf_op jit(solution)/shard_map/all_to_all | solution.py:17
  61.2 2.4 broadcast_select_fusion.1
  63.6 0.0 all-reduce.4.cloned.1.call-update
  63.7 0.0 reduce-scatter.5.cloned.1.call-start
  63.7 173.3 %all-reduce.4.cloned.1.call-done = (bf16[1024,1024]{1,0:T(8,128)(2,1)}, bf16[1024,1024]{1,0:T(8,128)(2,1)}) async-done(((bf16[1024,1024]{1,0:T(8,128)(2,1)}, bf16[1024,1024]{1,0:T(8,128)(2,1)}), (bf16[1024,1024]{1,0:T(8,128)(2,1)}, bf16[1024,1024]{1,0:T(8,128)(2,1)})) %all-reduce.4.cloned.1.call-update) | async-done | bytes 4194320 | tf_op jit(solution)/shard_map/psum | solution.py:13
  237.0 5.9 %convolution_bitcast_fusion = f32[1024,1024]{0,1:T(8,128)} fusion(bf16[1024,1024]{1,0:T(8,128)(2,1)} %get-tuple-element.7, bf16[1024,1024]{1,0:T(8,128)(2,1)S(1)} %bitcast.35), kind=kOutput, calls=%fused_computation | convolution fusion | flops 2147483648 | bytes 8388608 | tf_op jit(solution)/shard_map/dot_general | solution.py:30
  242.9 0.0 reduce-scatter.5.cloned.1.call-update
  243.0 0.0 reduce-scatter.3.cloned.1.call-start
  243.0 6.1 %convolution_bitcast_fusion.1 = f32[1024,1024]{0,1:T(8,128)} fusion(bf16[1024,1024]{1,0:T(8,128)(2,1)} %get-tuple-element.8, bf16[1024,1024]{1,0:T(8,128)(2,1)S(1)} %bitcast.36), kind=kOutput, calls=%fused_computation.1 | convolution fusion | flops 2147483648 | bytes 8388608 | tf_op jit(solution)/shard_map/dot_general | solution.py:30
  249.1 0.0 copy-start.3
  249.1 0.0 copy-start.2
  249.1 0.0 reduce-scatter.3.cloned.1.call-update
  249.1 0.7 copy-done.3
  249.8 12.6 %all-reduce = (s32[1024]{0:T(1024)S(1)}, s32[1024]{0:T(1024)S(1)}) all-reduce(s32[1024]{0:T(1024)S(1)} %get-tuple-element.16, s32[1024]{0:T(1024)S(1)} %get-tuple-element.17), channel_id=1, replica_groups=mesh['seq'=16,'kmer'=2] {'seq'}, use_global_device_ids=true, to_apply=%region_5.6 | all-reduce | flops 2048 | bytes 16384 | tf_op jit(solution)/shard_map/psum | solution.py:13
  262.4 0.1 dynamic_slice.12
  262.5 0.1 dynamic_slice.14
  262.5 0.0 copy-done.2
  262.5 0.1 broadcast_bitcast_fusion
  262.6 0.0 reduce-scatter.5.cloned.1.call-done
  262.6 7.2 %reduce-scatter.3.cloned.1.call-done = f32[1024,512]{0,1:T(8,128)} async-done(((f32[1024,1024]{0,1:T(8,128)}), f32[1024,512]{0,1:T(8,128)}) %reduce-scatter.3.cloned.1.call-update) | async-done | bytes 2097168 | tf_op jit(solution)/shard_map/reduce_scatter | solution.py:31
  269.9 0.5 broadcast_in_dim.19
  270.4 0.0 copy-start
  270.4 0.0 copy-start.1
  270.4 0.5 broadcast_in_dim.17
  270.9 1.1 copy-done
  272.0 0.6 copy-done.1
  272.6 0.8 fusion
  273.5 0.2 pad_maximum_fusion
  273.7 4.0 %copy.10 = bf16[1024,2,512]{2,1,0:T(2,128)(2,1)} copy(bf16[1024,2,512]{0,2,1:T(8,128)(2,1)S(1)} %pad_maximum_fusion) | data formatting | bytes 4194304 | tf_op jit(solution)/shard_map/stack | solution.py:39
  (4 shorter events, 0.0 us)
Async XLA Ops:
  9.7 8.5 %copy-start.4 = (s32[2]{0:T(128)S(1)}, s32[2]{0:T(128)}, u32[]{:S(2)}) copy-start(s32[2]{0:T(128)} %param.6) | copy-start | bytes 28
  9.7 51.5 %all-to-all-start = ((bf16[64,16,1024]{2,0,1:T(8,128)(2,1)}), bf16[64,16,1024]{2,0,1:T(8,128)(2,1)S(1)}, u32[]{:S(2)}, u32[]{:S(2)}) async-start(bf16[64,16,1024]{2,0,1:T(8,128)(2,1)} %bitcast.37), calls=%async_computation | async-start | bytes 4194304 | tf_op jit(solution)/shard_map/all_to_all | solution.py:17
  18.1 218.9 %all-reduce.4.cloned.1.call-start = ((), (), s32[]{:S(2)}) async-start(), calls=%async_computation.5 | async-start | bytes 8388608 | tf_op jit(solution)/shard_map/psum | solution.py:13
  63.7 199.0 %reduce-scatter.5.cloned.1.call-start = ((), (), s32[]{:S(2)}) async-start(), calls=%async_computation.4 | async-start | bytes 6291456 | tf_op jit(solution)/shard_map/reduce_scatter | solution.py:31
  243.0 26.9 %reduce-scatter.3.cloned.1.call-start = ((), (), s32[]{:S(2)}) async-start(), calls=%async_computation.3 | async-start | bytes 6291456 | tf_op jit(solution)/shard_map/reduce_scatter | solution.py:31
  249.1 0.7 copy-start.3
  249.1 13.5 %copy-start.2 = (s32[2,8,8]{2,1,0:T(8,128)S(1)}, s32[2,8,8]{2,1,0:T(8,128)}, u32[]{:S(2)}) copy-start(s32[2,8,8]{2,1,0:T(8,128)} %param.7) | copy-start | bytes 1540
  270.4 1.6 copy-start
  270.4 2.2 copy-start.1
Sparse Core Ops, SparseCore 0:
  63.8 173.2 all-reduce.3
  243.1 11.0 reduce-scatter.4
  256.4 13.4 reduce-scatter.2
where the time goes:
time: 285 us; the launch traced here: 284 us
  waiting for transfers between devices  222 us (78%)
  between operations  14.4 us (5%)
  blocking collectives  12.6 us (4%)
  matrix products  12 us (4%)
  local copies, waits for them, and re-layouts  11.4 us (4%)
  starting transfers between devices  8.57 us (3%)
  other arithmetic  3.47 us (1%)
    psum x1, waiting for transfers between devices, broadcast(): return lax.psum(block, axis)  173 us
    all_to_all x1, waiting for transfers between devices, shards(): lax.all_to_all(profiles, 'seq', split_axis=1, concat_axis=0, tiled=True)  41.2 us
    psum x1, blocking collectives, broadcast(): return lax.psum(block, axis)  12.6 us
    dot_general x2, matrix products, shards(): lax.dot_general(local, panel, contract, preferred_element_type=jnp.float32)  12 us
    all_to_all x1, starting transfers between devices, shards(): lax.all_to_all(profiles, 'seq', split_axis=1, concat_axis=0, tiled=True)  8.44 us
    reduce_scatter x2, waiting for transfers between devices, shards(): lax.psum_scatter(partial_value, 'kmer', scatter_dimension=1, tiled=True)  7.26 us
  transfers between devices with their start and end apart: 4, of which 3 were waited for; matrix products, arithmetic and copies ran while one was open for 2% of the time, Pallas kernels for 0%

commit v1 on v0

--- a/solution.py
+++ b/solution.py
@@ -1,11 +1,16 @@
+import functools
+
 import jax
 import jax.numpy as jnp
 from jax import lax
+from jax.experimental import pallas as pl
+from jax.experimental.pallas import tpu as pltpu
 from jax.sharding import PartitionSpec as P
 
 KM = 2048
 BLK = 128
 SECTIONS = 2
+MESH = pl.DeviceIdType.MESH
 
 
 def broadcast(block, axis, source):
@@ -39,8 +44,307 @@
     return jnp.stack(outs, axis=1)
 
 
+PLANES, ACROSS = 4, 4
+
+
+def kernel(
+    prof_hbm, mine_hbm, lens_hbm, owners, mask, out, prof, panel, local, acc, lens, lens_all,
+    in_sem, ex_sem, p_send, p_recv, l_send, l_recv, f_send, len_send, len_recv,
+):
+    n = PLANES * ACROSS
+    feats = prof.shape[0]
+    size = local.shape[1]
+    half = size // 2
+    me, core = lax.axis_index("seq"), lax.axis_index("kmer")
+    sib = 1 - core
+    z, xy = lax.div(me, ACROSS), lax.rem(me, ACROSS)
+    y, x = lax.div(xy, 2), lax.rem(xy, 2)
+    xn = me + 1 - 2 * x
+    yn = me + 2 * (1 - 2 * y)
+    high = lax.div(z, 2)
+    order = [z, z + 1 - 2 * lax.rem(z, 2), 2 - high, 3 - 3 * high]
+    shift = [(p - z) * ACROSS for p in order]
+    inner = jnp.logical_or(z == 1, z == 2)
+    pair, middle = me + shift[1], me + ACROSS * (3 - 2 * z)
+
+    def rows(place, c):
+        return pl.ds(pl.multiple_of((place * 2 + c) * feats, feats), feats)
+
+    def columns(start, length):
+        return pl.ds(pl.multiple_of(start, length), length)
+
+    def piece(place, c, slot, to):
+        at = panel.at[rows(place, c)]
+        i = place * 2 + c
+        return pltpu.make_async_remote_copy(
+            src_ref=at, dst_ref=at, send_sem=p_send.at[i * 4 + slot], recv_sem=p_recv.at[i],
+            device_id=(to, core), device_id_type=MESH,
+        )
+
+    def block_to(to):
+        return pltpu.make_async_remote_copy(
+            src_ref=prof.at[:, columns(to * size, size)], dst_ref=local.at[rows(me, core)],
+            send_sem=l_send.at[to], recv_sem=l_recv.at[me * 2 + core],
+            device_id=(to, core), device_id_type=MESH,
+        )
+
+    def lens_to(to):
+        return pltpu.make_async_remote_copy(
+            src_ref=lens.at[core], dst_ref=lens_all.at[me],
+            send_sem=len_send.at[to], recv_sem=len_recv.at[me],
+            device_id=(to, core), device_id_type=MESH,
+        )
+
+    def hand_over(place, own=False):
+        at = local.at[rows(place, core)]
+        return pltpu.make_async_remote_copy(
+            src_ref=prof.at[:, columns(me * size, size)] if own else at, dst_ref=at,
+            send_sem=f_send.at[place], recv_sem=l_recv.at[place * 2 + core],
+            device_id=(me, sib), device_id_type=MESH,
+        )
+
+    def local_arrived(place, c):
+        at = local.at[rows(place, c)]
+        pltpu.make_async_remote_copy(
+            src_ref=at, dst_ref=at, send_sem=f_send.at[place], recv_sem=l_recv.at[place * 2 + c],
+            device_id=(me, sib), device_id_type=MESH,
+        ).wait_recv()
+
+    load = pltpu.make_async_copy(prof_hbm, prof, in_sem.at[0])
+    load.start()
+    load_lens = pltpu.make_async_copy(lens_hbm, lens, in_sem.at[1])
+    load_lens.start()
+
+    load_mine = pltpu.make_async_copy(mine_hbm.at[core], panel.at[rows(me, core)], in_sem.at[2])
+    load_mine.start()
+
+    barrier = pltpu.get_barrier_semaphore()
+
+    @pl.loop(1, n)
+    def _(i):
+        pl.semaphore_signal(
+            barrier, inc=1, device_id=(lax.rem(me + i, n), core), device_id_type=MESH
+        )
+
+    pl.semaphore_signal(barrier, inc=1, device_id=(me, sib), device_id_type=MESH)
+    load.wait()
+    load_lens.wait()
+    load_mine.wait()
+    local[rows(me, core), :] = prof[:, columns(me * size, size)]
+    lens_all[me] = lens[core]
+    pl.semaphore_wait(barrier, n)
+
+    exchange = pltpu.make_async_remote_copy(
+        src_ref=mine_hbm.at[sib], dst_ref=panel.at[rows(me, core)], send_sem=ex_sem,
+        recv_sem=p_recv.at[me * 2 + core], device_id=(me, sib), device_id_type=MESH,
+    )
+    exchange.start()
+
+    def spread(q, c):
+        place = me + shift[q]
+        if q == 0:
+            piece(place, c, 0, pair).start()
+
+            @pl.when(inner)
+            def _():
+                piece(place, c, 1, middle).start()
+        else:
+            piece(place, c, 0, pair).wait_recv()
+
+            @pl.when(inner)
+            def _():
+                piece(place, c, 0, middle if q == 1 else pair).start()
+
+        piece(place, c, 2, xn).start()
+        piece(place, c, 3, yn).start()
+
+    def cross(q):
+        piece(xn + shift[q], 0, 3, yn).wait_recv()
+        piece(xn + shift[q], 0, 3, yn).start()
+        piece(yn + shift[q], 1, 2, xn).wait_recv()
+        piece(yn + shift[q], 1, 2, xn).start()
+
+    def pass_on(q):
+        for j in range(ACROSS):
+            if q == 0 and j == 0:
+                continue
+            place = order[q] * ACROSS + lax.rem(xy + j, ACROSS)
+            local_arrived(place, core)
+            hand_over(place).start()
+
+    def multiply(q):
+        for j in range(ACROSS):
+            local_arrived(order[q] * ACROSS + lax.rem(xy + j, ACROSS), sib)
+        piece(xn + shift[q], 1, 3, yn).wait_recv()
+        piece(yn + shift[q], 0, 3, yn).wait_recv()
+        diagonal = xn + yn - me + shift[q]
+        for c in range(2):
+            piece(diagonal, c, 0, yn).wait_recv()
+        deep = ACROSS * 2 * feats
+        span = pl.ds(pl.multiple_of(order[q] * deep, deep), deep)
+
+        @pl.loop(0, size // 256)
+        def _(i):
+            at = pl.ds(pl.multiple_of(i * 256, 256), 256)
+            value = lax.dot_general(
+                local[span, at], panel[span, :], (((0,), (0,)), ((), ())),
+                preferred_element_type=jnp.float32,
+            )
+            if q == 0:
+                acc[at, :] = value
+            else:
+                acc[at, :] += value
+
+    place = me
+    piece(place, core, 0, pair).start()
+
+    @pl.when(inner)
+    def _():
+        piece(place, core, 1, middle).start()
+
+    piece(place, core, 2, xn).start()
+    piece(place, core, 3, yn).start()
+    hand_over(me, own=True).start()
+    piece(place, sib, 0, pair).wait_recv()
+    spread(0, sib)
+
+    for j in range(ACROSS):
+        for q in (2, 3, 1, 0):
+            if q == 0 and j == 0:
+                continue
+            to = order[q] * ACROSS + lax.rem(xy + j, ACROSS)
+            block_to(to).start()
+            lens_to(to).start()
+
+    for q in range(1, PLANES):
+        spread(q, 0)
+        spread(q, 1)
+        cross(q - 1)
+        if q >= 2:
+            pass_on(q - 2)
+        if q >= 3:
+            multiply(q - 3)
+    cross(3)
+    pass_on(2)
+    multiply(1)
+    pass_on(3)
+    multiply(2)
+
+    @pl.loop(1, n)
+    def _(i):
+        other = lax.rem(me + i, n)
+        pltpu.make_async_remote_copy(
+            src_ref=lens.at[core], dst_ref=lens_all.at[other],
+            send_sem=len_send.at[other], recv_sem=len_recv.at[other],
+            device_id=(other, core), device_id_type=MESH,
+        ).wait_recv()
+
+    multiply(3)
+
+    scale = 256.0 / jnp.sqrt(jnp.float32(KM))
+    for t in range(SECTIONS):
+        col_len = jnp.zeros(lens_all.shape[1:], jnp.int32)
+        for i in range(n):
+            off = owners[t] - i
+            col_len += jnp.maximum(1 - off * off, 0) * lens_all[i]
+        col_len = col_len.astype(jnp.float32)
+
+        @pl.loop(0, 2)
+        def _(h):
+            for r in range(size // BLK // 2):
+                i = h * (size // BLK // 2) + r
+                row = lens[h, r:r + 1, :].astype(jnp.float32)
+                row_len = jnp.broadcast_to(row, (BLK, BLK)).T
+                at = pl.ds(pl.multiple_of(i * BLK, BLK), BLK)
+                for j in range(half // BLK):
+                    spot = slice(j * BLK, (j + 1) * BLK)
+                    norm = scale * lax.rsqrt(row_len * col_len[j:j + 1, :])
+                    scored = mask[t, i, core * (half // BLK) + j].astype(jnp.float32)
+                    raw = acc[at, t * half + j * BLK:t * half + (j + 1) * BLK]
+                    out[t, at, spot] = (raw * norm * scored).astype(out.dtype)
+
+    exchange.wait_send()
+    for c in range(2):
+        piece(me, c, 0, pair).wait_send()
+        piece(me, c, 2, xn).wait_send()
+        piece(me, c, 3, yn).wait_send()
+        for q in range(1, PLANES):
+            piece(me + shift[q], c, 2, xn).wait_send()
+            piece(me + shift[q], c, 3, yn).wait_send()
+
+    @pl.when(inner)
+    def _():
+        for c in range(2):
+            piece(me, c, 1, middle).wait_send()
+            for q in range(1, PLANES):
+                piece(me + shift[q], c, 0, pair).wait_send()
+
+    for q in range(PLANES):
+        piece(xn + shift[q], 0, 3, yn).wait_send()
+        piece(yn + shift[q], 1, 2, xn).wait_send()
+    hand_over(me, own=True).wait_send()
+
+    @pl.loop(1, n)
+    def _(i):
+        other = lax.rem(me + i, n)
+        block_to(other).wait_send()
+        lens_to(other).wait_send()
+        hand_over(other).wait_send()
+
+
+def fused(profiles, lengths, owners, block_mask):
+    n = PLANES * ACROSS
+    feats, size = profiles.shape[0], lengths.shape[0]
+    half = size // 2
+    lens = lengths.reshape(2, half // BLK, BLK)
+    parts = [
+        lax.dynamic_slice_in_dim(profiles, owners[t] * size, size, 1).reshape(feats, 2, half)
+        for t in range(SECTIONS)
+    ]
+    mine = jnp.concatenate(parts, axis=2).transpose(1, 0, 2)
+    out = pl.pallas_call(
+        kernel,
+        out_shape=jax.ShapeDtypeStruct((SECTIONS, size, half), jnp.bfloat16),
+        in_specs=[
+            pl.BlockSpec(memory_space=pl.ANY),
+            pl.BlockSpec(memory_space=pl.ANY),
+            pl.BlockSpec(memory_space=pl.ANY),
+            pl.BlockSpec(memory_space=pltpu.SMEM),
+            pl.BlockSpec(memory_space=pltpu.SMEM),
+        ],
+        out_specs=pl.BlockSpec(memory_space=pltpu.VMEM),
+        scratch_shapes=[
+            pltpu.VMEM(profiles.shape, jnp.bfloat16),
+            pltpu.VMEM((KM, size), jnp.bfloat16),
+            pltpu.VMEM((KM, size), jnp.bfloat16),
+            pltpu.VMEM((size, size), jnp.float32),
+            pltpu.VMEM(lens.shape, jnp.int32),
+            pltpu.VMEM((n,) + lens.shape[1:], jnp.int32),
+            pltpu.SemaphoreType.DMA((3,)),
+            pltpu.SemaphoreType.DMA,
+            pltpu.SemaphoreType.DMA((n * 2 * 4,)),
+            pltpu.SemaphoreType.DMA((n * 2,)),
+            pltpu.SemaphoreType.DMA((n,)),
+            pltpu.SemaphoreType.DMA((n * 2,)),
+            pltpu.SemaphoreType.DMA((n,)),
+            pltpu.SemaphoreType.DMA((n,)),
+            pltpu.SemaphoreType.DMA((n,)),
+        ],
+        compiler_params=pltpu.CompilerParams(
+            collective_id=0, has_side_effects=True, vmem_limit_bytes=48 * 1024 * 1024
+        ),
+        cost_estimate=pl.CostEstimate(
+            flops=2 * KM * size * size, bytes_accessed=8 * 1024 * 1024, transcendentals=size * size
+        ),
+    )(profiles, mine, lens, owners, block_mask)
+    return out.transpose(1, 0, 2)
+
+
 def solution(mesh):
     placed = (P(("seq", "kmer"), None), P("seq"), P(), P(None, "seq", None))
+    n, cores = mesh.shape["seq"], mesh.shape["kmer"]
+    fits = n == PLANES * ACROSS and cores == 2
     return jax.shard_map(
-        shards, mesh=mesh, in_specs=placed, out_specs=P("seq", None, "kmer"), check_vma=False
+        fused if fits else shards,
+        mesh=mesh, in_specs=placed, out_specs=P("seq", None, "kmer"), check_vma=False,
     )

time: 285 us -> 98.3 us (0.34)
  waiting for transfers between devices: 222 us -> 0 us
  Pallas kernels: 0 us -> 87.2 us
  between operations: 14.4 us -> 1.39 us
  blocking collectives: 12.6 us -> 0 us
  matrix products: 12 us -> 0 us
  starting transfers between devices: 8.57 us -> 0 us
  other arithmetic: 3.47 us -> 0.02 us
    psum x1 -> x0, waiting for transfers between devices: 173 us -> none  [broadcast(): return lax.psum(block, axis)]
    pallas_call x0 -> x1, Pallas kernels: none -> 87.2 us  [fused(): pl.pallas_call(kernel, out_shape=jax.ShapeDtypeStruct((SECTIONS, size, ha...]
    all_to_all x1 -> x0, waiting for transfers between devices: 41.2 us -> none  [shards(): lax.all_to_all(profiles, 'seq', split_axis=1, concat_axis=0, tiled=True)]
    psum x1 -> x0, blocking collectives: 12.6 us -> none  [broadcast(): return lax.psum(block, axis)]
    dot_general x2 -> x0, matrix products: 12 us -> none  [shards(): lax.dot_general(local, panel, contract, preferred_element_type=jnp.float32)]
    all_to_all x1 -> x0, starting transfers between devices: 8.44 us -> none  [shards(): lax.all_to_all(profiles, 'seq', split_axis=1, concat_axis=0, tiled=True)]
    reduce_scatter x2 -> x0, waiting for transfers between devices: 7.26 us -> none  [shards(): lax.psum_scatter(partial_value, 'kmer', scatter_dimension=1, tiled=True)]
    another operation x1 -> x0, local copies, waits for them, and re-layouts: 4.05 us -> none  [shards(): return jnp.stack(outs, axis=1)]
  transfers between devices with their start and end apart: 4 -> 0, of which waited for: 3 -> 0; matrix products, arithmetic and copies ran while one was open for 2% -> 0% of each run, Pallas kernels for 0% -> 0%
where the time goes in v1:
time: 98.3 us; the launch traced here: 98.1 us
  Pallas kernels  87.2 us (89%)
  local copies, waits for them, and re-layouts  9.5 us (10%)
  between operations  1.39 us (1%)
    pallas_call x1, Pallas kernels, fused(): pl.pallas_call(kernel, out_shape=jax.ShapeDtypeStruct((SECTIONS, size, ha...  87.2 us
    unnamed x8, local copies, waits for them, and re-layouts  3.62 us
    transpose x1, local copies, waits for them, and re-layouts, fused(): return out.transpose(1, 0, 2)  3.48 us

profile of v1, /device:TPU:0, one launch (start us, length us, event | category | flops | bytes accessed | tf_op | source)
XLA Modules:
  0.0 98.1 jit_solution(8770076845335030780)
XLA Ops:
  0.0 1.4 %fusion = (s32[1]{0:T(128)}, s32[1]{0:T(128)}) fusion(s32[2]{0:T(128)} %owners.1), kind=kLoop, calls=%fused_computation.5 | loop fusion | bytes 16 | tf_op jit(solution)/shard_map/slice | solution.py:301
  2.7 1.0 %constant_dynamic-slice_fusion.1 = (bf16[64,1024]{1,0:T(8,128)(2,1)S(1)}, bf16[64,1024]{1,0:T(8,128)(2,1)S(1)}) fusion(bf16[64,16384]{1,0:T(8,128)(2,1)} %prof_hbm.1, s32[]{:T(128)S(6)} %select_n.6, s32[]{:T(128)S(6)} %select_n.7), kind=kLoop, calls=%fused_computation.4 | loop fusion | bytes 524296 | tf_op jit(solution)/shard_map/dynamic_slice | solution.py:301
  3.8 0.0 copy-start
  3.8 1.6 %copy-done = bf16[64,16384]{1,0:T(8,128)(2,1)S(1)} copy-done((bf16[64,16384]{1,0:T(8,128)(2,1)S(1)}, bf16[64,16384]{1,0:T(8,128)(2,1)}, u32[]{:S(2)}) %copy-start) | copy-done | bytes 2097176
  5.4 0.0 copy-start.1
  5.4 0.7 copy-done.1
  6.0 0.0 copy-start.2
  6.0 0.7 copy-done.2
  6.7 0.0 copy-start.3
  6.7 0.7 copy-done.3
  7.4 87.2 %shard_map.46 = bf16[2,1024,512]{2,1,0:T(8,128)(2,1)S(1)} custom-call(bf16[64,16384]{1,0:T(8,128)(2,1)S(1)} %copy-done, bf16[2,64,1024]{2,1,0:T(8,128)(2,1)S(1)} %maximum_bitcast_fusion.mine_hbm, s32[2,4,128]{2,1,0:T(4,128)S(1)} %bitcast.13, s32[2]{0:T(128)S(1)} %copy-done.1, s32[2,8,8]{2,1,0:T(8,128)S(1)} %copy-done.2), custom_call_target="tpu_custom_call" | custom-call | flops 4294967296 | bytes 8388608 | tf_op jit(solution)/shard_map/pallas_call | solution.py:305
  94.6 3.5 %copy.8 = bf16[1024,2,512]{2,1,0:T(2,128)(2,1)} copy(bf16[1024,2,512]{2,0,1:T(8,128)(2,1)S(1)} %bitcast.12) | data formatting | bytes 4194304 | tf_op jit(solution)/shard_map/transpose | solution.py:340
  (2 shorter events, 0.0 us)
Async XLA Ops:
  3.8 1.6 %copy-start = (bf16[64,16384]{1,0:T(8,128)(2,1)S(1)}, bf16[64,16384]{1,0:T(8,128)(2,1)}, u32[]{:S(2)}) copy-start(bf16[64,16384]{1,0:T(8,128)(2,1)} %prof_hbm.1) | copy-start | bytes 6291460
  5.4 0.7 copy-start.1
  6.0 0.7 copy-start.2
  6.7 0.7 copy-start.3

commit v2 on v1

--- a/solution.py
+++ b/solution.py
@@ -48,7 +48,7 @@
 
 
 def kernel(
-    prof_hbm, mine_hbm, lens_hbm, owners, mask, out, prof, panel, local, acc, lens, lens_all,
+    prof_hbm, first, second, lens_hbm, owners, mask, out, prof, ex, panel, local, acc, lens, lens_all,
     in_sem, ex_sem, p_send, p_recv, l_send, l_recv, f_send, len_send, len_recv,
 ):
     n = PLANES * ACROSS
@@ -115,8 +115,18 @@
     load_lens = pltpu.make_async_copy(lens_hbm, lens, in_sem.at[1])
     load_lens.start()
 
-    load_mine = pltpu.make_async_copy(mine_hbm.at[core], panel.at[rows(me, core)], in_sem.at[2])
-    load_mine.start()
+    own_half, other_half = columns(core * half, half), columns(sib * half, half)
+    load_mine = []
+    for t, part in enumerate((first, second)):
+        spot = pl.ds(t * half, half)
+        load_mine.append(pltpu.make_async_copy(
+            part.at[:, own_half], panel.at[rows(me, core), spot], in_sem.at[2 + t]
+        ))
+        load_mine.append(pltpu.make_async_copy(
+            part.at[:, other_half], ex.at[:, spot], in_sem.at[4 + t]
+        ))
+    for step in load_mine:
+        step.start()
 
     barrier = pltpu.get_barrier_semaphore()
 
@@ -129,13 +139,14 @@
     pl.semaphore_signal(barrier, inc=1, device_id=(me, sib), device_id_type=MESH)
     load.wait()
     load_lens.wait()
-    load_mine.wait()
+    for step in load_mine:
+        step.wait()
     local[rows(me, core), :] = prof[:, columns(me * size, size)]
     lens_all[me] = lens[core]
     pl.semaphore_wait(barrier, n)
 
     exchange = pltpu.make_async_remote_copy(
-        src_ref=mine_hbm.at[sib], dst_ref=panel.at[rows(me, core)], send_sem=ex_sem,
+        src_ref=ex, dst_ref=panel.at[rows(me, core)], send_sem=ex_sem,
         recv_sem=p_recv.at[me * 2 + core], device_id=(me, sib), device_id_type=MESH,
     )
     exchange.start()
@@ -298,14 +309,16 @@
     half = size // 2
     lens = lengths.reshape(2, half // BLK, BLK)
     parts = [
-        lax.dynamic_slice_in_dim(profiles, owners[t] * size, size, 1).reshape(feats, 2, half)
+        lax.dynamic_slice(
+            profiles, (0, owners[t] * size), (feats, size), allow_negative_indices=False
+        )
         for t in range(SECTIONS)
     ]
-    mine = jnp.concatenate(parts, axis=2).transpose(1, 0, 2)
     out = pl.pallas_call(
         kernel,
         out_shape=jax.ShapeDtypeStruct((SECTIONS, size, half), jnp.bfloat16),
         in_specs=[
+            pl.BlockSpec(memory_space=pl.ANY),
             pl.BlockSpec(memory_space=pl.ANY),
             pl.BlockSpec(memory_space=pl.ANY),
             pl.BlockSpec(memory_space=pl.ANY),
@@ -315,12 +328,13 @@
         out_specs=pl.BlockSpec(memory_space=pltpu.VMEM),
         scratch_shapes=[
             pltpu.VMEM(profiles.shape, jnp.bfloat16),
+            pltpu.VMEM((feats, size), jnp.bfloat16),
             pltpu.VMEM((KM, size), jnp.bfloat16),
             pltpu.VMEM((KM, size), jnp.bfloat16),
             pltpu.VMEM((size, size), jnp.float32),
             pltpu.VMEM(lens.shape, jnp.int32),
             pltpu.VMEM((n,) + lens.shape[1:], jnp.int32),
-            pltpu.SemaphoreType.DMA((3,)),
+            pltpu.SemaphoreType.DMA((6,)),
             pltpu.SemaphoreType.DMA,
             pltpu.SemaphoreType.DMA((n * 2 * 4,)),
             pltpu.SemaphoreType.DMA((n * 2,)),
@@ -336,7 +350,7 @@
         cost_estimate=pl.CostEstimate(
             flops=2 * KM * size * size, bytes_accessed=8 * 1024 * 1024, transcendentals=size * size
         ),
-    )(profiles, mine, lens, owners, block_mask)
+    )(profiles, *parts, lens, owners, block_mask)
     return out.transpose(1, 0, 2)
 
 

time: 98.3 us -> 98 us (level)
  no operation moved by 1% of the time
where the time goes in v2:
time: 98 us; the launch traced here: 97.7 us
  Pallas kernels  87.1 us (89%)
  local copies, waits for them, and re-layouts  9.4 us (10%)
  between operations  1.24 us (1%)
    pallas_call x1, Pallas kernels, fused(): pl.pallas_call(kernel, out_shape=jax.ShapeDtypeStruct((SECTIONS, size, ha...  87.1 us
    unnamed x8, local copies, waits for them, and re-layouts  3.62 us
    transpose x1, local copies, waits for them, and re-layouts, fused(): return out.transpose(1, 0, 2)  3.48 us

profile of v2, /device:TPU:0, one launch (start us, length us, event | category | flops | bytes accessed | tf_op | source)
XLA Modules:
  0.0 97.7 jit_solution(17202544937962020823)
XLA Ops:
  0.0 1.3 %fusion = (s32[1]{0:T(128)}, s32[1]{0:T(128)}) fusion(s32[2]{0:T(128)} %owners.1), kind=kLoop, calls=%fused_computation.2 | loop fusion | bytes 16 | tf_op jit(solution)/shard_map/slice | solution.py:313
  2.5 1.0 %constant_dynamic-slice_fusion = (bf16[64,1024]{1,0:T(8,128)(2,1)S(1)}, bf16[64,1024]{1,0:T(8,128)(2,1)S(1)}) fusion(bf16[64,16384]{1,0:T(8,128)(2,1)} %prof_hbm.1, s32[]{:T(128)} %bitcast.1, s32[]{:T(128)} %bitcast), kind=kLoop, calls=%fused_computation | loop fusion | bytes 524296 | tf_op jit(solution)/shard_map/dynamic_slice | solution.py:312
  3.5 0.0 copy-start
  3.5 1.6 %copy-done = bf16[64,16384]{1,0:T(8,128)(2,1)S(1)} copy-done((bf16[64,16384]{1,0:T(8,128)(2,1)S(1)}, bf16[64,16384]{1,0:T(8,128)(2,1)}, u32[]{:S(2)}) %copy-start) | copy-done | bytes 2097176
  5.1 0.0 copy-start.1
  5.1 0.7 copy-done.1
  5.8 0.0 copy-start.2
  5.8 0.7 copy-done.2
  6.5 0.0 copy-start.3
  6.5 0.7 copy-done.3
  7.2 87.1 %shard_map.46 = bf16[2,1024,512]{2,1,0:T(8,128)(2,1)S(1)} custom-call(bf16[64,16384]{1,0:T(8,128)(2,1)S(1)} %copy-done, bf16[64,1024]{1,0:T(8,128)(2,1)S(1)} %get-tuple-element.6.first, bf16[64,1024]{1,0:T(8,128)(2,1)S(1)} %get-tuple-element.5.second, s32[2,4,128]{2,1,0:T(4,128)S(1)} %bitcast.5, s32[2]{0:T(128)S(1)} %copy-done.1, s32[2,8,8]{2,1,0:T(8,128)S(1)} %copy-done.2), custom_call_target="tpu_custom_call" | custom-call | flops 4294967296 | bytes 8388608 | tf_op jit(solution)/shard_map/pallas_call | solution.py:317
  94.2 3.5 %copy.5 = bf16[1024,2,512]{2,1,0:T(2,128)(2,1)} copy(bf16[1024,2,512]{2,0,1:T(8,128)(2,1)S(1)} %bitcast.4) | data formatting | bytes 4194304 | tf_op jit(solution)/shard_map/transpose | solution.py:354
Async XLA Ops:
  3.5 1.6 %copy-start = (bf16[64,16384]{1,0:T(8,128)(2,1)S(1)}, bf16[64,16384]{1,0:T(8,128)(2,1)}, u32[]{:S(2)}) copy-start(bf16[64,16384]{1,0:T(8,128)(2,1)} %prof_hbm.1) | copy-start | bytes 6291460
  5.1 0.7 copy-start.1
  5.8 0.7 copy-start.2
  6.5 0.7 copy-start.3

commit v3 on v2

--- a/solution.py
+++ b/solution.py
@@ -219,18 +219,23 @@
     piece(place, sib, 0, pair).wait_recv()
     spread(0, sib)
 
-    for j in range(ACROSS):
-        for q in (2, 3, 1, 0):
-            if q == 0 and j == 0:
-                continue
-            to = order[q] * ACROSS + lax.rem(xy + j, ACROSS)
-            block_to(to).start()
-            lens_to(to).start()
+    def send_blocks(planes):
+        for j in range(ACROSS):
+            for q in planes:
+                if q == 0 and j == 0:
+                    continue
+                to = order[q] * ACROSS + lax.rem(xy + j, ACROSS)
+                block_to(to).start()
+                lens_to(to).start()
+
+    send_blocks((3, 2))
 
     for q in range(1, PLANES):
         spread(q, 0)
         spread(q, 1)
         cross(q - 1)
+        if q == 1:
+            send_blocks((0, 1))
         if q >= 2:
             pass_on(q - 2)
         if q >= 3:

time: 98 us -> 97.8 us (level)
  no operation moved by 1% of the time
where the time goes in v3:
time: 97.8 us; the launch traced here: 97.6 us
  Pallas kernels  86.9 us (89%)
  local copies, waits for them, and re-layouts  9.4 us (10%)
  between operations  1.24 us (1%)
    pallas_call x1, Pallas kernels, fused(): pl.pallas_call(kernel, out_shape=jax.ShapeDtypeStruct((SECTIONS, size, ha...  86.9 us
    unnamed x8, local copies, waits for them, and re-layouts  3.62 us
    transpose x1, local copies, waits for them, and re-layouts, fused(): return out.transpose(1, 0, 2)  3.48 us

profile of v3, /device:TPU:0, one launch (start us, length us, event | category | flops | bytes accessed | tf_op | source)
XLA Modules:
  0.0 97.6 jit_solution(11553239128334690948)
XLA Ops:
  0.0 1.3 %fusion = (s32[1]{0:T(128)}, s32[1]{0:T(128)}) fusion(s32[2]{0:T(128)} %owners.1), kind=kLoop, calls=%fused_computation.2 | loop fusion | bytes 16 | tf_op jit(solution)/shard_map/slice | solution.py:318
  2.5 1.0 %constant_dynamic-slice_fusion = (bf16[64,1024]{1,0:T(8,128)(2,1)S(1)}, bf16[64,1024]{1,0:T(8,128)(2,1)S(1)}) fusion(bf16[64,16384]{1,0:T(8,128)(2,1)} %prof_hbm.1, s32[]{:T(128)} %bitcast.1, s32[]{:T(128)} %bitcast), kind=kLoop, calls=%fused_computation | loop fusion | bytes 524296 | tf_op jit(solution)/shard_map/dynamic_slice | solution.py:317
  3.5 0.0 copy-start
  3.5 1.6 %copy-done = bf16[64,16384]{1,0:T(8,128)(2,1)S(1)} copy-done((bf16[64,16384]{1,0:T(8,128)(2,1)S(1)}, bf16[64,16384]{1,0:T(8,128)(2,1)}, u32[]{:S(2)}) %copy-start) | copy-done | bytes 2097176
  5.1 0.0 copy-start.1
  5.1 0.7 copy-done.1
  5.8 0.0 copy-start.2
  5.8 0.7 copy-done.2
  6.5 0.0 copy-start.3
  6.5 0.7 copy-done.3
  7.2 86.9 %shard_map.46 = bf16[2,1024,512]{2,1,0:T(8,128)(2,1)S(1)} custom-call(bf16[64,16384]{1,0:T(8,128)(2,1)S(1)} %copy-done, bf16[64,1024]{1,0:T(8,128)(2,1)S(1)} %get-tuple-element.6.first, bf16[64,1024]{1,0:T(8,128)(2,1)S(1)} %get-tuple-element.5.second, s32[2,4,128]{2,1,0:T(4,128)S(1)} %bitcast.5, s32[2]{0:T(128)S(1)} %copy-done.1, s32[2,8,8]{2,1,0:T(8,128)S(1)} %copy-done.2), custom_call_target="tpu_custom_call" | custom-call | flops 4294967296 | bytes 8388608 | tf_op jit(solution)/shard_map/pallas_call | solution.py:322
  94.1 3.5 %copy.5 = bf16[1024,2,512]{2,1,0:T(2,128)(2,1)} copy(bf16[1024,2,512]{2,0,1:T(8,128)(2,1)S(1)} %bitcast.4) | data formatting | bytes 4194304 | tf_op jit(solution)/shard_map/transpose | solution.py:359
Async XLA Ops:
  3.5 1.6 %copy-start = (bf16[64,16384]{1,0:T(8,128)(2,1)S(1)}, bf16[64,16384]{1,0:T(8,128)(2,1)}, u32[]{:S(2)}) copy-start(bf16[64,16384]{1,0:T(8,128)(2,1)} %prof_hbm.1) | copy-start | bytes 6291460
  5.1 0.7 copy-start.1
  5.8 0.7 copy-start.2
  6.5 0.7 copy-start.3
